TPU v7x, 128 devices: a whole 4x4x4 slice. The times are simulated.
128 devices in a mesh: role: 2 (over y_hi), dev: 64 (over z, x, y_lo, core).
Axes of the slice: x: 4, y: 4 (y_hi: 2, y_lo: 2; y = y_hi * 2 + y_lo), z: 4, core: 2. Of those that a mesh axis runs over, the one named last changes fastest.
Arguments:
- tokens: bfloat16 [65536, 1024], P(('role', 'dev')), may hold values from -6 to 6
- expert_ids: int32 [65536, 1], P(('role', 'dev')), may hold values from 0 to 127; in each aligned block of 512 rows (0 to 511, 512 to 1023, ...) at most 8 rows name the same one
- w_qkv: bfloat16 [1024, 3072], P(('role', 'dev')), may hold values from -2 to 2
- w_attn_out: bfloat16 [1024, 1024], P(('role', 'dev')), may hold values from -0.1875 to 0.1875
- gain_attn: bfloat16 [1024], replicated, may hold values from 0.5 to 1.5
- gain_expert: bfloat16 [1024], replicated, may hold values from 0.5 to 1.5
- router: bfloat16 [1024, 128], replicated, may hold values from -0.375 to 0.375
- expert_in: bfloat16 [128, 1024, 2816], P(('role', 'dev')), may hold values from -0.1875 to 0.1875
- expert_out: bfloat16 [128, 2816, 1024], P(('role', 'dev')), may hold values from -0.109375 to 0.109375
- capacity: int32 [128], replicated, may hold values from 256 to 1023
- swap_list: int32 [32], replicated, may hold values from 0 to 63, as said below
Outputs:
- mixed: bfloat16 [65536, 1024], P(('role', 'dev'))
Inputs may be any that keep to these rules, and one draw needn't show every extreme that they name: `expert_ids`: in the rows of one device no expert is named more than 8 times, a bound that some block reaches. `swap_list`: entries are distinct.
All inputs are finite; a program needn't handle non-finite values.
Results may differ from a plain program's by a relative error of at most 0.0052.
Values may be sent and summed in bfloat16 or wider, within the bound.
A program may use at most 128 MiB of HBM per device.

v0:
```python
import jax
import jax.numpy as jnp
from jax import lax
from jax.sharding import PartitionSpec as P

HEADS = 16


def entering(value, axis, join, neutral):
    count, mine = (lax.axis_size(axis), lax.axis_index(axis))
    pieces = lax.all_gather(value, axis)
    total = jnp.full_like(value, 0) + jnp.asarray(neutral, value.dtype)

    def turn(position, total):
        longer = join(total, pieces[position])
        return jnp.where(position < mine, longer, total)

    return lax.fori_loop(0, count - 1, turn, total)


def swapped(value, axis, stride):
    mask = 2**stride
    pairs = [(source, source ^ mask) for source in range(lax.axis_size(axis))]
    return lax.ppermute(value, axis, pairs)


def rms_scale(values, gain_vector):
    mean_sq = jnp.mean(values * values, axis=-1, keepdims=True)
    return values * lax.rsqrt(mean_sq + 1e-06) * gain_vector.astype(jnp.float32)


def self_attend(qkv_rows, head_count):
    row_count = qkv_rows.shape[0]
    model_width = qkv_rows.shape[1] // 3
    head_size = model_width // head_count
    queries = qkv_rows[:, :model_width].reshape(row_count, head_count, head_size)
    keys_all = qkv_rows[:, model_width : 2 * model_width].reshape(row_count, head_count, head_size)
    values = qkv_rows[:, 2 * model_width :].reshape(row_count, head_count, head_size)
    scores = jnp.einsum(
        "shd,thd->hst", queries, keys_all, preferred_element_type=jnp.float32
    ) * head_size ** (-0.5)
    row_max = jnp.max(scores, axis=-1, keepdims=True)
    weights = jnp.exp(scores - row_max)
    soft_weights = (weights / jnp.sum(weights, axis=-1, keepdims=True)).astype(jnp.bfloat16)
    context = jnp.einsum("hst,thd->shd", soft_weights, values, preferred_element_type=jnp.float32)
    return context.reshape(row_count, model_width).astype(jnp.bfloat16)


def add_counts(earlier, later):
    return earlier + later


def shards(
    tokens,
    expert_ids,
    w_qkv,
    w_attn_out,
    gain_attn,
    gain_expert,
    router,
    expert_in,
    expert_out,
    capacity,
    swap_list,
):
    seq_len, model_width = tokens.shape
    residual = tokens.astype(jnp.float32)
    normed = rms_scale(residual, gain_attn).astype(jnp.bfloat16)
    columns = normed
    qkv_rows = jnp.dot(
        columns,
        lax.all_gather(w_qkv, ("role", "dev"), axis=0, tiled=True),
        preferred_element_type=jnp.float32,
    ).astype(jnp.bfloat16)
    context = self_attend(qkv_rows, HEADS)
    columns = context
    attended = jnp.dot(
        columns,
        lax.all_gather(w_attn_out, ("role", "dev"), axis=0, tiled=True),
        preferred_element_type=jnp.float32,
    )
    hidden = residual + attended
    normed_ffn = rms_scale(hidden, gain_expert).astype(jnp.bfloat16)
    logits = jnp.dot(normed_ffn, router, preferred_element_type=jnp.float32)
    experts_all = router.shape[1]
    dev_count = lax.axis_size("dev")
    chosen = expert_ids[:, 0]
    expert_range = jnp.arange(experts_all, dtype=jnp.int32)
    match = chosen[:, None] == expert_range[None, :]
    gate = jax.nn.sigmoid(jnp.sum(jnp.where(match, logits, 0.0), axis=1))
    counts = jnp.sum(match.astype(jnp.int32), axis=0)
    before = entering(counts, ("role", "dev"), add_counts, jnp.zeros_like(counts))
    row_ids = lax.broadcasted_iota(jnp.int32, (seq_len, seq_len), 0)
    col_ids = lax.broadcasted_iota(jnp.int32, (seq_len, seq_len), 1)
    strict_lower = (col_ids < row_ids).astype(jnp.bfloat16)
    rank_table = jnp.dot(
        strict_lower, match.astype(jnp.bfloat16), preferred_element_type=jnp.float32
    )
    local_rank = jnp.sum(jnp.where(match, rank_table, 0.0), axis=1).astype(jnp.int32)
    position = local_rank + jnp.sum(jnp.where(match, before[None, :], 0), axis=1)
    flagged = jnp.any(swap_list[:, None] == jnp.arange(dev_count, dtype=jnp.int32)[None, :], axis=0)
    dev_index = expert_range % dev_count
    role_index = expert_range // dev_count
    flag_expert = jnp.any(
        (dev_index[:, None] == jnp.arange(dev_count, dtype=jnp.int32)[None, :]) & flagged[None, :],
        axis=1,
    )
    location = jnp.where(flag_expert, (1 - role_index) * dev_count + dev_index, expert_range)
    cap_expert = jnp.sum(
        jnp.where(location[:, None] == expert_range[None, :], capacity[None, :], 0), axis=1
    )
    limit = jnp.sum(jnp.where(match, cap_expert[None, :], 0), axis=1)
    kept = position < limit
    slot_rows = max(2, 2 * seq_len // experts_all)
    partner_in, partner_out = swapped((expert_in, expert_out), "role", 0)
    mine_swaps = jnp.any(swap_list == lax.axis_index("dev"))
    weight_in = jnp.where(mine_swaps, partner_in[0], expert_in[0])
    weight_out = jnp.where(mine_swaps, partner_out[0], expert_out[0])
    token_dest = jnp.sum(jnp.where(match, location[None, :], 0), axis=1)
    slot_index = token_dest * slot_rows + local_rank
    buffer = (
        jnp.zeros((experts_all * slot_rows, model_width), jnp.bfloat16)
        .at[slot_index]
        .set(normed_ffn)
    )
    buffer = buffer.reshape(experts_all, slot_rows, model_width)
    received = lax.all_to_all(buffer, ("role", "dev"), split_axis=0, concat_axis=0, tiled=True)
    flat_rows = received.reshape(-1, model_width)
    activ = jnp.maximum(
        jnp.dot(flat_rows, weight_in, preferred_element_type=jnp.float32), 0.0
    ).astype(jnp.bfloat16)
    produced = jnp.dot(activ, weight_out, preferred_element_type=jnp.float32).astype(jnp.bfloat16)
    returned = lax.all_to_all(
        produced.reshape(received.shape), ("role", "dev"), split_axis=0, concat_axis=0, tiled=True
    )
    picked = returned.reshape(-1, model_width)[slot_index].astype(jnp.float32)
    mixed = hidden + jnp.where(kept, gate, 0.0)[:, None] * picked
    return mixed.astype(jnp.bfloat16)


def solution(mesh):
    return jax.shard_map(
        shards,
        mesh=mesh,
        in_specs=(
            P(("role", "dev"), None),
            P(("role", "dev"), None),
            P(("role", "dev"), None),
            P(("role", "dev"), None),
            P(),
            P(),
            P(),
            P(("role", "dev"), None, None),
            P(("role", "dev"), None, None),
            P(),
            P(),
        ),
        out_specs=P(("role", "dev"), None),
        check_vma=False,
    )
```

profile of v0, /device:TPU:1, one launch (start us, length us, event | category | flops | bytes accessed | tf_op | source)
XLA Modules:
  0.0 754.5 jit_solution(13278155795753660415)
XLA Ops:
  7.3 3.8 collective-permute-start.1
  12.1 1.1 fusion.27
  13.2 1.5 fusion.15
  14.7 412.8 %all-gather.1 = s32[128,1,128]{2,1,0:T(1,128)S(1)} all-gather(s32[1,1,128]{2,1,0:T(1,128)S(1)} %bitcast.57), channel_id=2, replica_groups=mesh['role'=2,'dev'=64] {'role','dev'}, dimensions={0}, use_global_device_ids=true | all-gather | bytes 66048 | tf_op jit(solution)/shard_map/all_gather | solution.py:11
  427.5 5.1 while.14
  433.3 16.4 %all-gather.5.cloned.1.call-done = bf16[1024,3072]{1,0:T(8,128)(2,1)} async-done(((bf16[8,3072]{1,0:T(8,128)(2,1)}), bf16[1024,3072]{1,0:T(8,128)(2,1)}) %all-gather.5.cloned.1.call-update) | async-done | bytes 6291472 | tf_op jit(solution)/shard_map/all_gather | solution.py:72
  449.7 6.6 convolution_convert_fusion
  456.2 1.3 fusion.43
  457.5 2.3 copy.24
  459.8 1.3 copy.25
  461.1 1.3 copy.26
  462.4 10.1 %fusion.44 = (f32[16,512]{1,0:T(8,128)S(1)}, f32[16,512,512]{1,2,0:T(8,128)}) fusion(bf16[512,16,64]{0,2,1:T(8,128)(2,1)S(1)} %bitcast.46, bf16[512,16,64]{0,2,1:T(8,128)(2,1)} %bitcast.47), kind=kOutput, calls=%fused_computation.75 | convolution fusion | flops 549454336 | bytes 18907136 | tf_op jit(solution)/shard_map/sub | solution.py:43
  472.5 8.3 %fusion.21 = bf16[16,64,512]{2,1,0:T(8,128)(2,1)} fusion(bf16[512,16,64]{0,2,1:T(8,128)(2,1)S(1)} %bitcast.45, f32[16,512,512]{1,2,0:T(8,128)} %get-tuple-element.115, f32[16,512]{1,0:T(8,128)S(1)} %get-tuple-element.114), kind=kOutput, calls=%fused_computation.32 | convolution fusion | flops 545783808 | bytes 18907136 | tf_op jit(solution)/shard_map/hst,thd->shd/dot_general | solution.py:45
  480.8 163.3 %all-gather.7.cloned.1.call-done = bf16[1024,1024]{1,0:T(8,128)(2,1)} async-done(((bf16[8,1024]{1,0:T(8,128)(2,1)}), bf16[1024,1024]{1,0:T(8,128)(2,1)}) %all-gather.7.cloned.1.call-update) | async-done | bytes 2097168 | tf_op jit(solution)/shard_map/all_gather | solution.py:79
  644.2 3.3 multiply_reduce_fusion.1
  647.5 4.2 scatter_custom_fusion
  651.7 7.1 all-to-all-start
  659.4 29.5 %all-to-all-done = bf16[128,8,1024]{2,1,0:T(8,128)(2,1)S(1)} async-done(((bf16[128,8,1024]{2,1,0:T(8,128)(2,1)}), bf16[128,8,1024]{2,1,0:T(8,128)(2,1)S(1)}, u32[]{:S(2)}, u32[]{:S(2)}) %all-to-all-start) | async-done | bytes 2097184 | tf_op jit(solution)/shard_map/all_to_all | solution.py:127
  688.9 18.3 %convert_bitcast_fusion = bf16[128,8,1024]{2,1,0:T(8,128)(2,1)} fusion(bf16[1,2816,1024]{2,1,0:T(8,128)(2,1)} %collective-permute-done.1, bf16[1,2816,1024]{2,1,0:T(8,128)(2,1)} %param.21, pred[]{:T(512)} %compare_reduce_fusion, bf16[1,1024,2816]{2,1,0:T(8,128)(2,1)} %collective-permute-done, bf16[1,1024,2816]{2,1,0:T(8,128)(2,1)} %param.20, ...), kind=kOutput, calls=%fused_computation.29 | convolution fusion | flops 11823742976 | bytes 27262976 | tf_op jit(solution)/shard_map/dot_general | solution.py:132
  707.2 5.4 all-to-all-start.1
  712.7 2.2 fusion.26
  714.9 27.9 %all-to-all-done.1 = bf16[128,8,1024]{2,1,0:T(8,128)(2,1)S(1)} async-done(((bf16[128,8,1024]{2,1,0:T(8,128)(2,1)}), bf16[128,8,1024]{2,1,0:T(8,128)(2,1)S(1)}, u32[]{:S(2)}, u32[]{:S(2)}) %all-to-all-start.1) | async-done | bytes 2097184 | tf_op jit(solution)/shard_map/all_to_all | solution.py:133
  742.8 2.0 gather_fusion
  744.8 2.9 add_convert_fusion
  (171 shorter events, 5.1 us)
Async XLA Ops:
  6.5 706.1 %copy-start = (bf16[1024,128]{1,0:T(8,128)(2,1)S(1)}, bf16[1024,128]{1,0:T(8,128)(2,1)}, u32[]{:S(2)}) copy-start(bf16[1024,128]{1,0:T(8,128)(2,1)} %param.19) | copy-start | bytes 786436
  6.5 426.5 %copy-start.5 = (s32[512,1]{0,1:T(1,128)S(1)}, s32[512,1]{0,1:T(1,128)}, u32[]{:S(2)}) copy-start(s32[512,1]{0,1:T(1,128)} %param.14) | copy-start | bytes 6148
  6.5 443.1 %copy-start.2 = (bf16[512,1024]{1,0:T(8,128)(2,1)S(1)}, bf16[512,1024]{1,0:T(8,128)(2,1)}, u32[]{:S(2)}) copy-start(bf16[512,1024]{1,0:T(8,128)(2,1)} %param.13) | copy-start | bytes 3145732
  6.5 426.1 %copy-start.9 = (s32[32]{0:T(128)S(1)}, s32[32]{0:T(128)}, u32[]{:S(2)}) copy-start(s32[32]{0:T(128)} %param.23) | copy-start | bytes 388
  6.5 426.3 %copy-start.8 = (s32[128]{0:T(128)S(1)}, s32[128]{0:T(128)}, u32[]{:S(2)}) copy-start(s32[128]{0:T(128)} %param.22) | copy-start | bytes 1540
  6.5 426.7 %copy-start.6 = (bf16[1024]{0:T(1024)(128)(2,1)S(1)}, bf16[1024]{0:T(1024)(128)(2,1)}, u32[]{:S(2)}) copy-start(bf16[1024]{0:T(1024)(128)(2,1)} %param.17) | copy-start | bytes 6148
  6.6 426.7 %copy-start.7 = (bf16[1024]{0:T(1024)(128)(2,1)S(1)}, bf16[1024]{0:T(1024)(128)(2,1)}, u32[]{:S(2)}) copy-start(bf16[1024]{0:T(1024)(128)(2,1)} %param.18) | copy-start | bytes 6148
  6.6 443.1 %all-gather.5.cloned.1.call-start = ((), (), s32[]{:S(2)}) async-start(), calls=%async_computation.2 | async-start | bytes 6340608 | tf_op jit(solution)/shard_map/all_gather | solution.py:72
  7.3 636.9 %all-gather.7.cloned.1.call-start = ((), (), s32[]{:S(2)}) async-start(), calls=%async_computation.3 | async-start | bytes 2113536 | tf_op jit(solution)/shard_map/all_gather | solution.py:79
  7.3 652.0 %collective-permute-start.1 = (bf16[1,2816,1024]{2,1,0:T(8,128)(2,1)}, bf16[1,2816,1024]{2,1,0:T(8,128)(2,1)}, u32[]{:S(2)}, u32[]{:S(2)}) collective-permute-start(bf16[1,2816,1024]{2,1,0:T(8,128)(2,1)} %param.21), channel_id=1, source_target_pairs={{0,64},{64,0},{1,65},{65,1},{2,66},{66,2},{3,67},{67,3},{4,68},{68... | collective-permute-start | bytes 17301512 | tf_op jit(solution)/shard_map/ppermute | solution.py:24
  11.2 648.2 %collective-permute-start = (bf16[1,1024,2816]{2,1,0:T(8,128)(2,1)}, bf16[1,1024,2816]{2,1,0:T(8,128)(2,1)}, u32[]{:S(2)}, u32[]{:S(2)}) collective-permute-start(bf16[1,1024,2816]{2,1,0:T(8,128)(2,1)} %param.20), channel_id=1, source_target_pairs={{0,64},{64,0},{1,65},{65,1},{2,66},{66,2},{3,67},{67,3},{4,68},{68... | collective-permute-start | bytes 17301512 | tf_op jit(solution)/shard_map/ppermute | solution.py:24
  461.1 1.3 copy-start.4
  462.4 10.1 %copy-start.3 = (bf16[512,1024]{0,1:T(8,128)(2,1)S(1)}, bf16[512,1024]{0,1:T(8,128)(2,1)}, u32[]{:S(2)}) copy-start(bf16[512,1024]{0,1:T(8,128)(2,1)} %copy.24) | copy-start | bytes 3145732
  647.4 4.2 copy-start.1
  651.7 37.2 %all-to-all-start = ((bf16[128,8,1024]{2,1,0:T(8,128)(2,1)}), bf16[128,8,1024]{2,1,0:T(8,128)(2,1)S(1)}, u32[]{:S(2)}, u32[]{:S(2)}) async-start(bf16[128,8,1024]{2,1,0:T(8,128)(2,1)} %bitcast.44), calls=%async_computation | async-start | bytes 4194304 | tf_op jit(solution)/shard_map/all_to_all | solution.py:127
  707.2 35.6 %all-to-all-start.1 = ((bf16[128,8,1024]{2,1,0:T(8,128)(2,1)}), bf16[128,8,1024]{2,1,0:T(8,128)(2,1)S(1)}, u32[]{:S(2)}, u32[]{:S(2)}) async-start(bf16[128,8,1024]{2,1,0:T(8,128)(2,1)} %convert_bitcast_fusion), calls=%async_computation.1 | async-start | bytes 4194304 | tf_op jit(solution)/shard_map/all_to_all | solution.py:133
Sparse Core Ops, SparseCore 0:
  9.1 440.4 all-gather.4
  451.4 192.7 all-gather.6
where the time goes:
time: 755 us
  blocking collectives  413 us (55%)
  waiting for transfers between devices  238 us (32%)
  matrix products  49.8 us (7%)
  starting transfers between devices  16.5 us (2%)
  between operations  13.6 us (2%)
  other arithmetic  12.8 us (2%)
  local copies, waits for them, and re-layouts  8.29 us (1%)
    all_gather x1, blocking collectives, entering(): pieces = lax.all_gather(value, axis)  413 us
    all_gather x1, waiting for transfers between devices, shards(): lax.all_gather(w_attn_out, ('role', 'dev'), axis=0, tiled=True)  163 us
    all_to_all x1, waiting for transfers between devices, shards(): lax.all_to_all(buffer, ('role', 'dev'), split_axis=0, concat_axis=0, tile...  29.5 us
    all_to_all x1, waiting for transfers between devices, shards(): lax.all_to_all(produced.reshape(received.shape), ('role', 'dev'), split_a...  27.9 us
    dot_general x1, matrix products, shards(): jnp.dot(activ, weight_out, preferred_element_type=jnp.float32)  18.3 us
    all_gather x1, waiting for transfers between devices, shards(): lax.all_gather(w_qkv, ('role', 'dev'), axis=0, tiled=True)  16.4 us
  transfers between devices with their start and end apart: 6, of which 4 were waited for; matrix products, arithmetic and copies ran while one was open for 6% of the time, Pallas kernels for 0%

commit v1 on v0

--- a/solution.py
+++ b/solution.py
@@ -1,9 +1,20 @@
+import functools
 import jax
 import jax.numpy as jnp
 from jax import lax
 from jax.sharding import PartitionSpec as P
 
 HEADS = 16
+
+
+def local_data_close(body, which_axis, axis_k):
+    by_place = []
+    for _ in range(lax.axis_size(which_axis)):
+        by_place.append(body)
+    return jnp.concatenate(lax.all_to_all(jnp.stack(by_place), which_axis, 0, 0), axis=axis_k)
+
+
+plan_object = functools.partial(local_data_close, which_axis=("role", "dev"), axis_k=0)
 
 
 def entering(value, axis, join, neutral):
@@ -67,11 +78,9 @@
     residual = tokens.astype(jnp.float32)
     normed = rms_scale(residual, gain_attn).astype(jnp.bfloat16)
     columns = normed
-    qkv_rows = jnp.dot(
-        columns,
-        lax.all_gather(w_qkv, ("role", "dev"), axis=0, tiled=True),
-        preferred_element_type=jnp.float32,
-    ).astype(jnp.bfloat16)
+    qkv_rows = jnp.dot(columns, plan_object(w_qkv), preferred_element_type=jnp.float32).astype(
+        jnp.bfloat16
+    )
     context = self_attend(qkv_rows, HEADS)
     columns = context
     attended = jnp.dot(

time: 755 us -> 656 us (0.87)
  waiting for transfers between devices: 238 us -> 57.9 us
  blocking collectives: 413 us -> 483 us
  starting transfers between devices: 16.5 us -> 25.2 us
    all_gather x1, waiting for transfers between devices: 163 us -> 0.01 us  [shards(): lax.all_gather(w_attn_out, ('role', 'dev'), axis=0, tiled=True)]
    all_gather x1, blocking collectives: 413 us -> 483 us  [entering(): pieces = lax.all_gather(value, axis)]
    all_gather x1 -> x0, waiting for transfers between devices: 16.4 us -> none  [shards(): lax.all_gather(w_qkv, ('role', 'dev'), axis=0, tiled=True)]
    all_to_all x0 -> x1, starting transfers between devices: none -> 11.9 us  [local_data_close(): lax.all_to_all(jnp.stack(by_place), which_axis, 0, 0)]
  transfers between devices with their start and end apart: 6 -> 6, of which waited for: 4 -> 2; matrix products, arithmetic and copies ran while one was open for 6% -> 7% of each run, Pallas kernels for 0% -> 0%
where the time goes in v1:
time: 656 us; the launch traced here: 655 us
  blocking collectives  483 us (74%)
  waiting for transfers between devices  57.9 us (9%)
  matrix products  49.7 us (8%)
  starting transfers between devices  25.2 us (4%)
  between operations  13.6 us (2%)
  local copies, waits for them, and re-layouts  11.8 us (2%)
  other arithmetic  10.9 us (2%)
    all_gather x1, blocking collectives, entering(): pieces = lax.all_gather(value, axis)  483 us
    all_to_all x1, waiting for transfers between devices, shards(): lax.all_to_all(buffer, ('role', 'dev'), split_axis=0, concat_axis=0, tile...  29.3 us
    all_to_all x1, waiting for transfers between devices, shards(): lax.all_to_all(produced.reshape(received.shape), ('role', 'dev'), split_a...  27.9 us
    dot_general x1, matrix products, shards(): jnp.dot(activ, weight_out, preferred_element_type=jnp.float32)  19 us
  transfers between devices with their start and end apart: 6, of which 2 were waited for; matrix products, arithmetic and copies ran while one was open for 7% of the time, Pallas kernels for 0%

profile of v1, /device:TPU:1, one launch (start us, length us, event | category | flops | bytes accessed | tf_op | source)
XLA Modules:
  0.0 655.3 jit_solution(17092298329519748894)
XLA Ops:
  6.5 4.3 stack.2
  10.9 11.9 %all-to-all-start = ((bf16[128,8,3072]{2,1,0:T(8,128)(2,1)}), bf16[128,8,3072]{2,1,0:T(8,128)(2,1)}, u32[]{:S(2)}, u32[]{:S(2)}) async-start(bf16[128,8,3072]{2,1,0:T(8,128)(2,1)} %stack.2), calls=%async_computation | async-start | bytes 12582912 | tf_op jit(solution)/shard_map/all_to_all | solution.py:14
  22.8 0.7 all-gather.4.cloned.1.call-update
  23.5 3.0 collective-permute-start.1
  26.7 483.4 %all-gather.1 = s32[128,1,128]{2,1,0:T(1,128)S(1)} all-gather(s32[1,1,128]{2,1,0:T(1,128)S(1)} %bitcast.61), channel_id=2, replica_groups=mesh['role'=2,'dev'=64] {'role','dev'}, dimensions={0}, use_global_device_ids=true | all-gather | bytes 66048 | tf_op jit(solution)/shard_map/all_gather | solution.py:22
  510.1 5.1 while.14
  516.5 6.6 %fusion.15 = bf16[512,3072]{1,0:T(8,128)(2,1)S(1)} fusion(bf16[128,8,3072]{2,1,0:T(8,128)(2,1)} %all-to-all-done, bf16[512,1024]{1,0:T(8,128)(2,1)S(1)} %copy-done.2, f32[1024]{0:T(1024)S(1)} %convert_element_type.62, f32[512]{0:T(512)S(1)} %add_rsqrt_fusion.1), kind=kOutput, calls=%fused_computation.21 | convolution fusion | flops 3224895488 | bytes 10491904 | tf_op jit(solution)/shard_map/dot_general | solution.py:81
  523.1 1.3 fusion.48
  524.3 2.3 copy.24
  526.6 1.3 copy.25
  527.9 0.5 copy.26
  528.5 10.1 %fusion.49 = (f32[16,512]{1,0:T(8,128)S(1)}, f32[16,512,512]{1,2,0:T(8,128)}) fusion(bf16[512,16,64]{0,2,1:T(8,128)(2,1)} %bitcast.50, bf16[512,16,64]{0,2,1:T(8,128)(2,1)S(1)} %bitcast.51), kind=kOutput, calls=%fused_computation.77 | convolution fusion | flops 549454336 | bytes 18907136 | tf_op jit(solution)/shard_map/sub | solution.py:54
  538.6 8.3 %fusion.26 = bf16[16,64,512]{2,1,0:T(8,128)(2,1)} fusion(bf16[512,16,64]{0,2,1:T(8,128)(2,1)S(1)} %bitcast.49, f32[16,512,512]{1,2,0:T(8,128)} %get-tuple-element.115, f32[16,512]{1,0:T(8,128)S(1)} %get-tuple-element.114), kind=kOutput, calls=%fused_computation.34 | convolution fusion | flops 545783808 | bytes 18907136 | tf_op jit(solution)/shard_map/hst,thd->shd/dot_general | solution.py:56
  546.9 3.3 multiply_reduce_fusion.1
  550.2 4.2 scatter_custom_fusion
  554.4 4.7 all-to-all-start.1
  559.2 0.6 compare_reduce_fusion
  559.8 29.3 %all-to-all-done.1 = bf16[128,8,1024]{2,1,0:T(8,128)(2,1)} async-done(((bf16[128,8,1024]{2,1,0:T(8,128)(2,1)}), bf16[128,8,1024]{2,1,0:T(8,128)(2,1)}, u32[]{:S(2)}, u32[]{:S(2)}) %all-to-all-start.1) | async-done | bytes 2097184 | tf_op jit(solution)/shard_map/all_to_all | solution.py:136
  589.1 19.0 %convert_bitcast_fusion = bf16[128,8,1024]{2,1,0:T(8,128)(2,1)} fusion(bf16[1,2816,1024]{2,1,0:T(8,128)(2,1)} %collective-permute-done.1, bf16[1,2816,1024]{2,1,0:T(8,128)(2,1)} %param.21, pred[]{:T(512)} %compare_reduce_fusion, bf16[1,1024,2816]{2,1,0:T(8,128)(2,1)} %collective-permute-done, bf16[1,1024,2816]{2,1,0:T(8,128)(2,1)} %param.20, ...), kind=kOutput, calls=%fused_computation.31 | convolution fusion | flops 11823742976 | bytes 27262976 | tf_op jit(solution)/shard_map/dot_general | solution.py:141
  608.0 5.4 all-to-all-start.2
  613.5 2.2 fusion.31
  615.7 27.9 %all-to-all-done.2 = bf16[128,8,1024]{2,1,0:T(8,128)(2,1)S(1)} async-done(((bf16[128,8,1024]{2,1,0:T(8,128)(2,1)}), bf16[128,8,1024]{2,1,0:T(8,128)(2,1)S(1)}, u32[]{:S(2)}, u32[]{:S(2)}) %all-to-all-start.2) | async-done | bytes 2097184 | tf_op jit(solution)/shard_map/all_to_all | solution.py:142
  643.6 2.0 gather_fusion
  645.6 2.9 add_convert_fusion
  (169 shorter events, 3.7 us)
Async XLA Ops:
  6.5 606.9 %copy-start = (bf16[1024,128]{1,0:T(8,128)(2,1)S(1)}, bf16[1024,128]{1,0:T(8,128)(2,1)}, u32[]{:S(2)}) copy-start(bf16[1024,128]{1,0:T(8,128)(2,1)} %param.19) | copy-start | bytes 786436
  10.8 15.8 %copy-start.4 = (s32[512,1]{0,1:T(1,128)S(1)}, s32[512,1]{0,1:T(1,128)}, u32[]{:S(2)}) copy-start(s32[512,1]{0,1:T(1,128)} %param.14) | copy-start | bytes 6148
  10.8 504.4 %copy-start.8 = (s32[32]{0:T(128)S(1)}, s32[32]{0:T(128)}, u32[]{:S(2)}) copy-start(s32[32]{0:T(128)} %param.23) | copy-start | bytes 388
  10.8 504.6 %copy-start.7 = (s32[128]{0:T(128)S(1)}, s32[128]{0:T(128)}, u32[]{:S(2)}) copy-start(s32[128]{0:T(128)} %param.22) | copy-start | bytes 1540
  10.8 505.3 %copy-start.2 = (bf16[512,1024]{1,0:T(8,128)(2,1)S(1)}, bf16[512,1024]{1,0:T(8,128)(2,1)}, u32[]{:S(2)}) copy-start(bf16[512,1024]{1,0:T(8,128)(2,1)} %param.13) | copy-start | bytes 3145732
  10.8 505.6 %copy-start.5 = (bf16[1024]{0:T(1024)(128)(2,1)S(1)}, bf16[1024]{0:T(1024)(128)(2,1)}, u32[]{:S(2)}) copy-start(bf16[1024]{0:T(1024)(128)(2,1)} %param.17) | copy-start | bytes 6148
  10.8 505.6 %copy-start.6 = (bf16[1024]{0:T(1024)(128)(2,1)S(1)}, bf16[1024]{0:T(1024)(128)(2,1)}, u32[]{:S(2)}) copy-start(bf16[1024]{0:T(1024)(128)(2,1)} %param.18) | copy-start | bytes 6148
  10.9 505.6 %all-to-all-start = ((bf16[128,8,3072]{2,1,0:T(8,128)(2,1)}), bf16[128,8,3072]{2,1,0:T(8,128)(2,1)}, u32[]{:S(2)}, u32[]{:S(2)}) async-start(bf16[128,8,3072]{2,1,0:T(8,128)(2,1)} %stack.2), calls=%async_computation | async-start | bytes 12582912 | tf_op jit(solution)/shard_map/all_to_all | solution.py:14
  22.8 524.1 %all-gather.4.cloned.1.call-start = ((), (), s32[]{:S(2)}) async-start(), calls=%async_computation.3 | async-start | bytes 2113536 | tf_op jit(solution)/shard_map/all_gather | solution.py:88
  23.5 536.3 %collective-permute-start.1 = (bf16[1,2816,1024]{2,1,0:T(8,128)(2,1)}, bf16[1,2816,1024]{2,1,0:T(8,128)(2,1)}, u32[]{:S(2)}, u32[]{:S(2)}) collective-permute-start(bf16[1,2816,1024]{2,1,0:T(8,128)(2,1)} %param.21), channel_id=1, source_target_pairs={{0,64},{64,0},{1,65},{65,1},{2,66},{66,2},{3,67},{67,3},{4,68},{68... | collective-permute-start | bytes 17301512 | tf_op jit(solution)/shard_map/ppermute | solution.py:35
  26.5 533.3 %collective-permute-start = (bf16[1,1024,2816]{2,1,0:T(8,128)(2,1)}, bf16[1,1024,2816]{2,1,0:T(8,128)(2,1)}, u32[]{:S(2)}, u32[]{:S(2)}) collective-permute-start(bf16[1,1024,2816]{2,1,0:T(8,128)(2,1)} %param.20), channel_id=1, source_target_pairs={{0,64},{64,0},{1,65},{65,1},{2,66},{66,2},{3,67},{67,3},{4,68},{68... | collective-permute-start | bytes 17301512 | tf_op jit(solution)/shard_map/ppermute | solution.py:35
  528.5 10.1 %copy-start.3 = (bf16[512,1024]{0,1:T(8,128)(2,1)S(1)}, bf16[512,1024]{0,1:T(8,128)(2,1)}, u32[]{:S(2)}) copy-start(bf16[512,1024]{0,1:T(8,128)(2,1)} %copy.24) | copy-start | bytes 3145732
  550.2 4.3 copy-start.1
  554.4 34.6 %all-to-all-start.1 = ((bf16[128,8,1024]{2,1,0:T(8,128)(2,1)}), bf16[128,8,1024]{2,1,0:T(8,128)(2,1)}, u32[]{:S(2)}, u32[]{:S(2)}) async-start(bf16[128,8,1024]{2,1,0:T(8,128)(2,1)} %bitcast.48), calls=%async_computation.1 | async-start | bytes 4194304 | tf_op jit(solution)/shard_map/all_to_all | solution.py:136
  608.0 35.6 %all-to-all-start.2 = ((bf16[128,8,1024]{2,1,0:T(8,128)(2,1)}), bf16[128,8,1024]{2,1,0:T(8,128)(2,1)S(1)}, u32[]{:S(2)}, u32[]{:S(2)}) async-start(bf16[128,8,1024]{2,1,0:T(8,128)(2,1)} %convert_bitcast_fusion), calls=%async_computation.2 | async-start | bytes 4194304 | tf_op jit(solution)/shard_map/all_to_all | solution.py:142
Sparse Core Ops, SparseCore 0:
  25.3 477.7 all-gather.3
